TPU v7x, 256 devices: a whole 4x4x8 slice. The times are simulated.
256 devices in a mesh: chan: 128 (over y, z, x_lo, core), tm: 2 (over x_hi).
Axes of the slice: x: 4 (x_hi: 2, x_lo: 2; x = x_hi * 2 + x_lo), y: 4, z: 8, core: 2. Of those that a mesh axis runs over, the one named last changes fastest.
Arguments:
- traces: float32 [4, 1024, 768], P('tm', 'chan'), may hold values from -6 to 6
- lengths: int32 [4], replicated, may hold values from 1 to 768, 2304 in all
- mask: int32 [1024], P('chan'), may hold values 0 or 1
Outputs:
- correlations: float32 [1024, 1024, 256], P(('chan', 'tm'))
Inputs may be any that keep to these rules, and one draw needn't show every extreme that they name: `lengths`: live samples of each sub-window; together they hold 2304 samples and the longest holds exactly 768.
All inputs are finite; a program needn't handle non-finite values. No bound on the sum of `mask` on one device may be relied on, other than what follows from the above.
Results may differ from a plain program's by a relative error of at most 0.0043.
Values may be sent and summed in bfloat16 or wider, within the bound.
No kernel may reach another device: no remote copies, remote signals or barrier semaphores. Data moves between devices by JAX's collectives and lax.ppermute only.
A program may use at most 128 MiB of HBM per device.

v0:
```python
import math
import jax
import jax.numpy as jnp
from jax import lax
from jax.sharding import PartitionSpec as P

NFFT = 1024
LAG = 128
F = 512


def dft_table(seg_len, nfft, nfreq):
    sample_idx = jnp.arange(seg_len, dtype=jnp.int32)
    freq_idx = jnp.arange(nfreq, dtype=jnp.int32)
    product = jnp.mod(sample_idx[:, None] * freq_idx[None, :], nfft).astype(jnp.float32)
    theta = product * (2.0 * math.pi / nfft)
    return jnp.concatenate([jnp.cos(theta), -jnp.sin(theta)], axis=1)


def lag_table(nfft, nfreq, max_lag, sub_total):
    freq_idx = jnp.arange(nfreq, dtype=jnp.int32)
    lag_idx = jnp.arange(2 * max_lag, dtype=jnp.int32) - max_lag
    product = jnp.mod(freq_idx[:, None] * lag_idx[None, :], nfft).astype(jnp.float32)
    phase = product * (2.0 * math.pi / nfft)
    weight = jnp.where(freq_idx == 0, 1.0, 2.0).astype(jnp.float32)[:, None] / math.sqrt(
        nfreq * sub_total
    )
    return jnp.concatenate([weight * jnp.cos(phase), -weight * jnp.sin(phase)], axis=0).astype(
        jnp.bfloat16
    )


def whiten_spectra(traces, lengths, mask):
    seg_len = traces.shape[2]
    live = (jnp.arange(seg_len, dtype=jnp.int32)[None, :] < lengths[:, None]).astype(jnp.float32)
    counted = lengths.astype(jnp.float32)
    average = jnp.sum(traces * live[:, None, :], axis=-1) / counted[:, None]
    centred = (traces - average[:, :, None]) * live[:, None, :]
    table = dft_table(seg_len, NFFT, F)
    spectrum = jnp.dot(
        centred.reshape(-1, seg_len),
        table,
        precision=lax.Precision.HIGHEST,
        preferred_element_type=jnp.float32,
    )
    spectrum = spectrum.reshape(traces.shape[0], traces.shape[1], 2 * F)
    power = spectrum[..., :F] ** 2 + spectrum[..., F:] ** 2
    level = jnp.mean(power, axis=-1, keepdims=True)
    factor = 1.0 / jnp.sqrt(power + 0.01 * level + 1e-06)
    factor = jnp.concatenate([factor, factor], axis=-1)
    return (spectrum * factor * mask.astype(jnp.float32)[None, :, None]).astype(jnp.bfloat16)


def cross_spectrum(own_spec, other_spec):
    nfreq = own_spec.shape[-1] // 2
    own_re = own_spec[..., :nfreq]
    own_im = own_spec[..., nfreq:]
    other_re = other_spec[..., :nfreq]
    other_im = other_spec[..., nfreq:]
    real_part = jnp.einsum(
        "kif,kjf->ijf", own_re, other_re, preferred_element_type=jnp.float32
    ) + jnp.einsum("kif,kjf->ijf", own_im, other_im, preferred_element_type=jnp.float32)
    imag_part = jnp.einsum(
        "kif,kjf->ijf", own_im, other_re, preferred_element_type=jnp.float32
    ) - jnp.einsum("kif,kjf->ijf", own_re, other_im, preferred_element_type=jnp.float32)
    return jnp.concatenate([real_part, imag_part], axis=-1).astype(jnp.bfloat16)


def place_lags(running, own_spec, incoming, begin_col, lag_matrix):
    column_count = incoming.shape[1]
    slab_cols = 128

    def one_slab(slab, offset, current):
        half_spectra = cross_spectrum(own_spec, slab)
        lag_values = jnp.dot(
            half_spectra.reshape(-1, half_spectra.shape[-1]),
            lag_matrix,
            preferred_element_type=jnp.float32,
        )
        lag_values = lag_values.reshape(own_spec.shape[1], slab.shape[1], lag_matrix.shape[1])
        return lax.dynamic_update_slice(
            current, lag_values, (jnp.int32(0), jnp.asarray(offset, jnp.int32), jnp.int32(0))
        )

    def loop_body(slab_index, current):
        slab = lax.dynamic_slice_in_dim(incoming, slab_index * slab_cols, slab_cols, 1)
        return one_slab(slab, begin_col + slab_index * slab_cols, current)

    return lax.fori_loop(0, column_count // slab_cols, loop_body, running)


def local(traces, lengths, mask):
    sub_count = traces.shape[0]
    own_rows = traces.shape[1]
    time_groups = lax.axis_size("tm")
    local_lengths = lax.dynamic_slice_in_dim(lengths, lax.axis_index("tm") * sub_count, sub_count)
    spectra = whiten_spectra(traces, local_lengths, mask)
    lag_matrix = lag_table(NFFT, F, LAG, sub_count * time_groups)
    channel_total = own_rows * lax.axis_size("chan")
    empty_lags = jnp.zeros((own_rows, channel_total, 2 * LAG), jnp.float32)
    partial_lags = place_lags(
        empty_lags,
        spectra,
        lax.all_gather(spectra, "chan", axis=1, tiled=True),
        jnp.int32(0),
        lag_matrix,
    )
    return lax.psum_scatter(partial_lags, "tm", scatter_dimension=0, tiled=True)


def solution(mesh):
    placed = (P("tm", "chan", None), P(), P("chan"))
    return jax.shard_map(
        local, mesh=mesh, in_specs=placed, out_specs=P(("chan", "tm"), None, None), check_vma=False
    )
```

profile of v0, /device:TPU:1, one launch (start us, length us, event | category | flops | bytes accessed | tf_op | source)
XLA Modules:
  0.0 562.4 jit_solution(10639168242448990964)
XLA Ops:
  6.5 6.2 %sine_negate_fusion = (f32[768,512]{1,0:T(8,128)S(1)}, f32[768,512]{1,0:T(8,128)S(1)}) fusion(), kind=kLoop, calls=%fused_computation.23 | loop fusion | flops 5898240 | bytes 3145728 | tf_op jit(solution)/shard_map/neg | solution.py:17
  19.0 216.1 %all-gather.2.cloned.1.call-done = bf16[2,1024,1024]{2,1,0:T(8,128)(2,1)} async-done(((bf16[2,8,1024]{2,1,0:T(8,128)(2,1)}), bf16[2,1024,1024]{2,1,0:T(8,128)(2,1)}) %all-gather.2.cloned.1.call-update) | async-done | bytes 4194320 | tf_op jit(solution)/shard_map/all_gather | solution.py:104
  235.1 3.9 broadcast_in_dim.8
  239.0 211.6 %while.13 = (s32[]{:T(128)}, f32[8,1024,256]{2,1,0:T(8,128)}, bf16[2,1024,1024]{2,1,0:T(8,128)(2,1)}, bf16[2,8,1024]{2,1,0:T(8,128)(2,1)S(1)}, bf16[1024,256]{1,...) while((s32[]{:T(128)}, f32[8,1024,256]{2,1,0:T(8,128)}, ...), condition=%wide.region_3.4_spmd, body=%wide.region_2.3_spmd.sunk | while | flops 551550976 | bytes 44761288 | solution.py:89
  252.0 3.0 copy.26
  257.2 2.9 copy.25
  260.1 3.7 fusion.83
  278.5 3.0 copy.26
  283.6 2.9 copy.25
  286.5 3.7 fusion.83
  304.9 3.0 copy.26
  310.0 2.9 copy.25
  313.0 3.7 fusion.83
  331.4 3.0 copy.26
  339.4 3.7 fusion.83
  357.8 3.0 copy.26
  365.9 3.7 fusion.83
  384.3 3.0 copy.26
  392.3 3.7 fusion.83
  410.7 3.0 copy.26
  418.8 3.7 fusion.83
  437.2 3.0 copy.26
  445.2 3.7 fusion.83
  450.6 104.9 %reduce-scatter.2.cloned.1.call-done = f32[4,1024,256]{2,1,0:T(8,128)} async-done(((f32[8,1024,256]{2,1,0:T(8,128)}), f32[4,1024,256]{2,1,0:T(8,128)}) %reduce-scatter.2.cloned.1.call-update) | async-done | bytes 4194320 | tf_op jit(solution)/shard_map/reduce_scatter | solution.py:108
  (151 shorter events, 155.3 us)
Async XLA Ops:
  6.5 6.2 %copy-start.4 = (s32[8]{0:T(128)S(1)}, s32[8]{0:T(128)}, u32[]{:S(2)}) copy-start(s32[8]{0:T(128)} %param.7) | copy-start | bytes 100
  6.5 6.2 %copy-start.3 = (s32[4]{0:T(128)S(1)}, s32[4]{0:T(128)}, u32[]{:S(2)}) copy-start(s32[4]{0:T(128)} %param.6) | copy-start | bytes 52
  6.5 6.4 %copy-start.2 = (f32[2,8,768]{2,1,0:T(8,128)S(1)}, f32[2,8,768]{2,1,0:T(8,128)}, u32[]{:S(2)}) copy-start(f32[2,8,768]{2,1,0:T(8,128)} %param.5) | copy-start | bytes 147460
  6.5 228.5 %all-gather.2.cloned.1.call-start = ((), (), s32[]{:S(2)}) async-start(), calls=%async_computation.1 | async-start | bytes 4227072 | tf_op jit(solution)/shard_map/all_gather | solution.py:104
  15.6 539.9 %reduce-scatter.2.cloned.1.call-start = ((), (), s32[]{:S(2)}) async-start(), calls=%async_computation.2 | async-start | bytes 12582912 | tf_op jit(solution)/shard_map/reduce_scatter | solution.py:108
  19.0 220.0 %copy-start = (bf16[2,8,1024]{2,1,0:T(8,128)(2,1)S(1)}, bf16[2,8,1024]{2,1,0:T(8,128)(2,1)}, u32[]{:S(2)}) copy-start(bf16[2,8,1024]{2,1,0:T(8,128)(2,1)} %fusion.28) | copy-start | bytes 98308
  260.1 3.7 copy-start.1
  286.5 3.7 copy-start.1
  313.0 3.7 copy-start.1
  339.4 3.7 copy-start.1
  365.9 3.7 copy-start.1
  392.3 3.7 copy-start.1
  418.8 3.7 copy-start.1
  445.2 3.7 copy-start.1
Sparse Core Ops, SparseCore 0:
  15.7 219.3 all-gather.1
  450.8 104.7 reduce-scatter.1
where the time goes:
time: 563 us; the launch traced here: 562 us
  waiting for transfers between devices  321 us (57%)
  local copies, waits for them, and re-layouts  104 us (18%)
  matrix products  83.3 us (15%)
  other arithmetic  39.8 us (7%)
  between operations  13.5 us (2%)
    all_gather x1, waiting for transfers between devices, local(): lax.all_gather(spectra, 'chan', axis=1, tiled=True)  216 us
    reduce_scatter x1, waiting for transfers between devices, local(): return lax.psum_scatter(partial_lags, 'tm', scatter_dimension=0, tiled=True)  105 us
    add x8, other arithmetic, cross_spectrum(): jnp.einsum('kif,kjf->ijf', own_re, other_re, preferred_element_type=jnp.f...  29.3 us
    dot_general x8, local copies, waits for them, and re-layouts, cross_spectrum(): jnp.einsum('kif,kjf->ijf', own_im, other_re, preferred_element_type=jnp.f...  24 us
    dot_general x8, local copies, waits for them, and re-layouts, cross_spectrum(): jnp.einsum('kif,kjf->ijf', own_im, other_im, preferred_element_type=jnp.f...  23.5 us
    dot_general x8, local copies, waits for them, and re-layouts, cross_spectrum(): jnp.einsum('kif,kjf->ijf', own_re, other_re, preferred_element_type=jnp.f...  23.4 us
    dot_general x8, matrix products, cross_spectrum(): jnp.einsum('kif,kjf->ijf', own_re, other_im, preferred_element_type=jnp.f...  17 us
    dot_general x8, matrix products, cross_spectrum(): jnp.einsum('kif,kjf->ijf', own_re, other_re, preferred_element_type=jnp.f...  17 us
  transfers between devices with their start and end apart: 2, of which 2 were waited for; matrix products, arithmetic and copies ran while one was open for 1% of the time, Pallas kernels for 0%

commit v1 on v0

--- a/solution.py
+++ b/solution.py
@@ -101,7 +101,9 @@
     partial_lags = place_lags(
         empty_lags,
         spectra,
-        lax.all_gather(spectra, "chan", axis=1, tiled=True),
+        jnp.concatenate(
+            lax.all_to_all(jnp.stack([spectra] * lax.axis_size("chan")), "chan", 0, 0), axis=1
+        ),
         jnp.int32(0),
         lag_matrix,
     )

time: 563 us -> 346 us (0.61)
  waiting for transfers between devices: 321 us -> 194 us
  local copies, waits for them, and re-layouts: 104 us -> 58.9 us
  matrix products: 83.3 us -> 49.8 us
  other arithmetic: 39.8 us -> 11.4 us
  starting transfers between devices: 0.22 us -> 15.5 us
    all_gather x1 -> x0, waiting for transfers between devices: 216 us -> none  [local(): lax.all_gather(spectra, 'chan', axis=1, tiled=True)]
    all_to_all x0 -> x1, waiting for transfers between devices: none -> 90.2 us  [local(): lax.all_to_all(jnp.stack([spectra] * lax.axis_size('chan')), 'chan', 0, 0)]
    add x8 -> x0, other arithmetic: 29.3 us -> none  [cross_spectrum(): jnp.einsum('kif,kjf->ijf', own_re, other_re, preferred_element_type=jnp.f...]
    dot_general x8, local copies, waits for them, and re-layouts: 23.4 us -> 1.46 us  [cross_spectrum(): jnp.einsum('kif,kjf->ijf', own_re, other_re, preferred_element_type=jnp.f...]
    dot_general x8, local copies, waits for them, and re-layouts: 24 us -> 7.16 us  [cross_spectrum(): jnp.einsum('kif,kjf->ijf', own_im, other_re, preferred_element_type=jnp.f...]
    dot_general x8, local copies, waits for them, and re-layouts: 23.5 us -> 7.24 us  [cross_spectrum(): jnp.einsum('kif,kjf->ijf', own_im, other_im, preferred_element_type=jnp.f...]
    all_to_all x0 -> x1, starting transfers between devices: none -> 15.3 us  [local(): lax.all_to_all(jnp.stack([spectra] * lax.axis_size('chan')), 'chan', 0, 0)]
    slice x48 -> x0, local copies, waits for them, and re-layouts: 13.9 us -> none  [the longest x16 9.97 us: cross_spectrum(): other_im = other_spec[..., nfreq:]]
where the time goes in v1:
time: 346 us; the launch traced here: 344 us
  waiting for transfers between devices  194 us (56%)
  local copies, waits for them, and re-layouts  58.9 us (17%)
  matrix products  49.8 us (14%)
  starting transfers between devices  15.5 us (4%)
  between operations  13.5 us (4%)
  other arithmetic  11.4 us (3%)
    reduce_scatter x1, waiting for transfers between devices, local(): return lax.psum_scatter(partial_lags, 'tm', scatter_dimension=0, tiled=True)  104 us
    all_to_all x1, waiting for transfers between devices, local(): lax.all_to_all(jnp.stack([spectra] * lax.axis_size('chan')), 'chan', 0, 0)  90.2 us
    all_to_all x1, starting transfers between devices, local(): lax.all_to_all(jnp.stack([spectra] * lax.axis_size('chan')), 'chan', 0, 0)  15.3 us
    dot_general x8, matrix products, cross_spectrum(): jnp.einsum('kif,kjf->ijf', own_im, other_im, preferred_element_type=jnp.f...  15.1 us
    dot_general x8, matrix products, one_slab(): jnp.dot(half_spectra.reshape(-1, half_spectra.shape[-1]), lag_matrix, pre...  13.8 us
    while x112, local copies, waits for them, and re-layouts  12.4 us
    dynamic_slice x16, local copies, waits for them, and re-layouts, loop_body(): lax.dynamic_slice_in_dim(incoming, slab_index * slab_cols, slab_cols, 1)  11.9 us
    dot_general x8, local copies, waits for them, and re-layouts, cross_spectrum(): jnp.einsum('kif,kjf->ijf', own_im, other_im, preferred_element_type=jnp.f...  7.24 us
  transfers between devices with their start and end apart: 2, of which 2 were waited for; matrix products, arithmetic and copies ran while one was open for 1% of the time, Pallas kernels for 0%

profile of v1, /device:TPU:1, one launch (start us, length us, event | category | flops | bytes accessed | tf_op | source)
XLA Modules:
  0.0 344.1 jit_solution(5840409792115888566)
XLA Ops:
  6.5 6.2 %sine_negate_fusion = (f32[768,512]{1,0:T(8,128)S(1)}, f32[768,512]{1,0:T(8,128)S(1)}) fusion(), kind=kLoop, calls=%fused_computation.27 | loop fusion | flops 5898240 | bytes 3145728 | tf_op jit(solution)/shard_map/neg | solution.py:17
  15.0 2.5 stack.2
  17.5 15.3 %all-to-all-start = ((bf16[128,2,8,1024]{3,2,1,0:T(8,128)(2,1)}), bf16[128,2,8,1024]{3,2,1,0:T(8,128)(2,1)}, u32[]{:S(2)}, u32[]{:S(2)}) async-start(bf16[128,2,8,1024]{3,2,1,0:T(8,128)(2,1)} %stack.2), calls=%async_computation | async-start | bytes 8388608 | tf_op jit(solution)/shard_map/all_to_all | solution.py:105
  33.5 2.3 multiply_convert_fusion.1
  36.6 90.2 %all-to-all-done = bf16[128,2,8,1024]{3,2,1,0:T(8,128)(2,1)} async-done(((bf16[128,2,8,1024]{3,2,1,0:T(8,128)(2,1)}), bf16[128,2,8,1024]{3,2,1,0:T(8,128)(2,1)}, u32[]{:S(2)}, u32[]{:S(2)}) %all-to-all-start) | async-done | bytes 4194336 | tf_op jit(solution)/shard_map/all_to_all | solution.py:105
  126.8 4.7 %copy.14 = bf16[128,2,8,1024]{3,2,0,1:T(8,128)(2,1)} copy(bf16[128,2,8,1024]{3,2,1,0:T(8,128)(2,1)} %all-to-all-done) | data formatting | bytes 8388608 | tf_op jit(solution)/shard_map/all_to_all | solution.py:105
  131.6 3.9 %broadcast_in_dim.8 = f32[8,1024,256]{2,1,0:T(8,128)} broadcast(f32[]{:T(128)} %constant.72.clone.1), dimensions={} | broadcast | bytes 8388612 | tf_op jit(solution)/shard_map/broadcast_in_dim | solution.py:100
  135.5 97.5 %while.13 = (s32[]{:T(128)}, f32[8,1024,256]{2,1,0:T(8,128)}, bf16[2,1024,1024]{2,1,0:T(8,128)(2,1)}, bf16[2,8,1024]{1,0,2:T(2,128)(2,1)S(1)}, bf16[1024,256]{1,...) while((s32[]{:T(128)}, f32[8,1024,256]{2,1,0:T(8,128)}, bf16[2,1024,1024]{2,1,0:T(8,128)(2,1)}, ...), condition=%wide.region_3.4_spmd, body=%wide.region_2.3_spmd.sunk | while | flops 548405248 | bytes 29491544 | solution.py:89
  140.9 1.9 fusion.101
  146.0 1.7 fusion.102
  153.0 1.9 fusion.101
  158.1 1.7 fusion.102
  165.2 1.9 fusion.101
  170.3 1.7 fusion.102
  177.4 1.9 fusion.101
  189.5 1.9 fusion.101
  194.6 1.7 fusion.102
  201.7 1.9 fusion.101
  206.8 1.7 fusion.102
  213.9 1.9 fusion.101
  219.0 1.7 fusion.102
  226.1 1.9 fusion.101
  231.2 1.7 fusion.102
  233.0 104.2 %reduce-scatter.2.cloned.1.call-done = f32[4,1024,256]{2,1,0:T(8,128)} async-done(((f32[8,1024,256]{2,1,0:T(8,128)}), f32[4,1024,256]{2,1,0:T(8,128)}) %reduce-scatter.2.cloned.1.call-update) | async-done | bytes 4194320 | tf_op jit(solution)/shard_map/reduce_scatter | solution.py:110
  (215 shorter events, 73.5 us)
Async XLA Ops:
  6.5 6.2 %copy-start.9 = (s32[8]{0:T(128)S(1)}, s32[8]{0:T(128)}, u32[]{:S(2)}) copy-start(s32[8]{0:T(128)} %param.7) | copy-start | bytes 100
  6.5 6.2 %copy-start.8 = (s32[4]{0:T(128)S(1)}, s32[4]{0:T(128)}, u32[]{:S(2)}) copy-start(s32[4]{0:T(128)} %param.6) | copy-start | bytes 52
  6.5 6.4 %copy-start.7 = (f32[2,8,768]{2,1,0:T(8,128)S(1)}, f32[2,8,768]{2,1,0:T(8,128)}, u32[]{:S(2)}) copy-start(f32[2,8,768]{2,1,0:T(8,128)} %param.5) | copy-start | bytes 147460
  17.5 109.3 %all-to-all-start = ((bf16[128,2,8,1024]{3,2,1,0:T(8,128)(2,1)}), bf16[128,2,8,1024]{3,2,1,0:T(8,128)(2,1)}, u32[]{:S(2)}, u32[]{:S(2)}) async-start(bf16[128,2,8,1024]{3,2,1,0:T(8,128)(2,1)} %stack.2), calls=%async_computation | async-start | bytes 8388608 | tf_op jit(solution)/shard_map/all_to_all | solution.py:105
  32.8 304.4 %reduce-scatter.2.cloned.1.call-start = ((), (), s32[]{:S(2)}) async-start(), calls=%async_computation.2 | async-start | bytes 12582912 | tf_op jit(solution)/shard_map/reduce_scatter | solution.py:110
  135.5 4.4 %copy-start = (bf16[2,8,1024]{1,0,2:T(2,128)(2,1)}, bf16[2,8,1024]{1,0,2:T(2,128)(2,1)S(1)}, u32[]{:S(2)}) copy-start(bf16[2,8,1024]{1,0,2:T(2,128)(2,1)S(1)} %get-tuple-element.175) | copy-start | bytes 98308 | tf_op jit(solution)/shard_map/while
  140.9 1.9 copy-start.4
  147.7 4.4 %copy-start = (bf16[2,8,1024]{1,0,2:T(2,128)(2,1)}, bf16[2,8,1024]{1,0,2:T(2,128)(2,1)S(1)}, u32[]{:S(2)}) copy-start(bf16[2,8,1024]{1,0,2:T(2,128)(2,1)S(1)} %get-tuple-element.175) | copy-start | bytes 98308 | tf_op jit(solution)/shard_map/while
  153.0 1.9 copy-start.4
  159.8 4.4 %copy-start = (bf16[2,8,1024]{1,0,2:T(2,128)(2,1)}, bf16[2,8,1024]{1,0,2:T(2,128)(2,1)S(1)}, u32[]{:S(2)}) copy-start(bf16[2,8,1024]{1,0,2:T(2,128)(2,1)S(1)} %get-tuple-element.175) | copy-start | bytes 98308 | tf_op jit(solution)/shard_map/while
  165.2 1.9 copy-start.4
  172.0 4.4 %copy-start = (bf16[2,8,1024]{1,0,2:T(2,128)(2,1)}, bf16[2,8,1024]{1,0,2:T(2,128)(2,1)S(1)}, u32[]{:S(2)}) copy-start(bf16[2,8,1024]{1,0,2:T(2,128)(2,1)S(1)} %get-tuple-element.175) | copy-start | bytes 98308 | tf_op jit(solution)/shard_map/while
  177.4 1.9 copy-start.4
  184.2 4.4 %copy-start = (bf16[2,8,1024]{1,0,2:T(2,128)(2,1)}, bf16[2,8,1024]{1,0,2:T(2,128)(2,1)S(1)}, u32[]{:S(2)}) copy-start(bf16[2,8,1024]{1,0,2:T(2,128)(2,1)S(1)} %get-tuple-element.175) | copy-start | bytes 98308 | tf_op jit(solution)/shard_map/while
  189.5 1.9 copy-start.4
  194.6 1.7 copy-start.1
  196.4 4.4 %copy-start = (bf16[2,8,1024]{1,0,2:T(2,128)(2,1)}, bf16[2,8,1024]{1,0,2:T(2,128)(2,1)S(1)}, u32[]{:S(2)}) copy-start(bf16[2,8,1024]{1,0,2:T(2,128)(2,1)S(1)} %get-tuple-element.175) | copy-start | bytes 98308 | tf_op jit(solution)/shard_map/while
  201.7 1.9 copy-start.4
  206.8 1.7 copy-start.1
  208.6 4.4 %copy-start = (bf16[2,8,1024]{1,0,2:T(2,128)(2,1)}, bf16[2,8,1024]{1,0,2:T(2,128)(2,1)S(1)}, u32[]{:S(2)}) copy-start(bf16[2,8,1024]{1,0,2:T(2,128)(2,1)S(1)} %get-tuple-element.175) | copy-start | bytes 98308 | tf_op jit(solution)/shard_map/while
  213.9 1.9 copy-start.4
  219.0 1.7 copy-start.1
  220.8 4.4 %copy-start = (bf16[2,8,1024]{1,0,2:T(2,128)(2,1)}, bf16[2,8,1024]{1,0,2:T(2,128)(2,1)S(1)}, u32[]{:S(2)}) copy-start(bf16[2,8,1024]{1,0,2:T(2,128)(2,1)S(1)} %get-tuple-element.175) | copy-start | bytes 98308 | tf_op jit(solution)/shard_map/while
  226.1 1.9 copy-start.4
  (37 other events, 41.9 us)
Sparse Core Ops, SparseCore 0:
  233.1 104.0 reduce-scatter.1
